TPU v7x, 32 devices: a whole 2x2x4 slice. The times are simulated.
32 devices in a mesh: grp: 2 (over x), aux: 16 (over z, y, core).
Axes of the slice: x: 2, y: 2, z: 4, core: 2. Of those that a mesh axis runs over, the one named last changes fastest.
Arguments:
- gamma_half: bfloat16 [32, 16, 9216], P(('grp', 'aux')), parts along dimension 0, may hold values from -6 to 6
- c_occ: bfloat16 [18432, 1000], P(('grp', 'aux')), parts along dimension 0, may hold values from -1.5 to 1.5
- integrals: bfloat16 [32, 16, 128, 128], P(('grp', 'aux')), parts along dimension 0, may hold values from -0.125 to 0.125
- occ_batch: int32 [32], P('grp'), parts along dimension 0, may hold values from 0 to 999, as said below
- kept_blocks: int32 [32, 2], P('grp'), parts along dimension 0, may hold values from 0 to 71, as said below
- block_owner: int32 [32], P('grp'), parts along dimension 0, may hold values from 0 to 15, as said below
Outputs:
- gamma_blocks: bfloat16 [64, 16, 128, 128], P(('grp', 'aux')), parts along dimension 0
- lagrangian: float32 [32, 9216], P('grp', 'aux'), parts along dimension 0
There are 2 independent parts, one for each index of `grp`. A program takes and returns all parts, laid end to end along the dimension named above; each array names one. Nothing has to cross between parts.
Inputs may be any that keep to these rules, and one draw needn't show every extreme that they name: `occ_batch`: distinct orbital indices. `kept_blocks`: distinct (row block, column block) pairs; the first min(16, 72) of them are diagonal pairs (r, r). `block_owner`: each owner is named by at most 2 blocks, and some owner by exactly 2.
All inputs are finite; a program needn't handle non-finite values.
Results may differ from a plain program's by a relative error of at most 0.001.
Values may be sent and summed in bfloat16 or wider, within the bound.
A program may use at most 64 MiB of HBM per device.

v0:
```python
import jax
import jax.numpy as jnp
from jax import lax
from jax.sharding import PartitionSpec as P

SLOTS = 2


def locate(block_owner, owner_count, slot_count):
    kept_count = block_owner.shape[0]
    indices = jnp.arange(kept_count, dtype=jnp.int32)
    earlier = (block_owner[:, None] == block_owner[None, :]) & (indices[None, :] < indices[:, None])
    slot_index = jnp.sum(earlier.astype(jnp.int32), axis=1)
    placed = block_owner * slot_count + slot_index
    target = jnp.arange(owner_count * slot_count, dtype=jnp.int32)
    matches = (placed[None, :] == target[:, None]).astype(jnp.int32)
    chosen = jnp.sum(matches * indices[None, :], axis=1)
    filled = jnp.sum(matches, axis=1)
    return (chosen, filled)


def body(gamma_half, c_occ, integrals, occ_batch, kept_blocks, block_owner):
    owner_count = lax.axis_size("aux")
    aux_dev, occ_width, basis = gamma_half.shape
    edge_size = integrals.shape[-1]
    block_count = basis // edge_size
    slot_count = SLOTS
    local_rows = jnp.take(c_occ, occ_batch, axis=1)
    occ_all = lax.all_gather(local_rows, "aux", axis=0, tiled=True)
    occ_tiles = occ_all.reshape(block_count, edge_size, occ_width)
    half_tiles = gamma_half.reshape(aux_dev, occ_width, block_count, edge_size).transpose(
        2, 0, 1, 3
    )
    chosen, filled = locate(block_owner, owner_count, slot_count)
    row_blocks = kept_blocks[:, 0]
    col_blocks = kept_blocks[:, 1]
    chosen_major = chosen.reshape(owner_count, slot_count).T.reshape(-1)
    filled_major = filled.reshape(owner_count, slot_count).T.reshape(-1)
    right_tiles = jnp.take(half_tiles, jnp.take(col_blocks, chosen_major), axis=0)
    right_tiles = right_tiles * filled_major[:, None, None, None].astype(jnp.bfloat16)
    factor = right_tiles.reshape(slot_count, owner_count, aux_dev, occ_width, edge_size)
    received = lax.all_to_all(factor, "aux", split_axis=1, concat_axis=1, tiled=True)
    received = received.reshape(slot_count, owner_count * aux_dev, occ_width, edge_size)
    my_index = lax.axis_index("aux")
    own_blocks = lax.dynamic_slice_in_dim(chosen, my_index * slot_count, slot_count)
    own_tiles = jnp.take(occ_tiles, jnp.take(row_blocks, own_blocks), axis=0)
    gamma_blocks = jnp.einsum(
        "sxb,spby->spxy", own_tiles, received, preferred_element_type=jnp.float32
    ).astype(jnp.bfloat16)
    kept_half = jnp.take(half_tiles, col_blocks, axis=0)
    pieces = jnp.einsum("pkxy,kpby->kbx", integrals, kept_half, preferred_element_type=jnp.float32)
    onehot = (row_blocks[None, :] == jnp.arange(block_count, dtype=jnp.int32)[:, None]).astype(
        jnp.float32
    )
    partial_value = jnp.einsum(
        "mk,kbx->bmx", onehot, pieces, precision=lax.Precision.HIGHEST
    ).reshape(occ_width, basis)
    lagrangian = lax.psum_scatter(partial_value, "aux", scatter_dimension=1, tiled=True)
    return (gamma_blocks, lagrangian)


def solution(mesh):
    return jax.shard_map(
        body,
        mesh=mesh,
        in_specs=(
            P(("grp", "aux"), None, None),
            P(("grp", "aux"), None),
            P(("grp", "aux"), None, None, None),
            P("grp"),
            P("grp", None),
            P("grp"),
        ),
        out_specs=(P(("grp", "aux"), None, None, None), P("grp", "aux")),
        check_vma=False,
    )
```

profile of v0, /device:TPU:0, one launch (start us, length us, event | category | flops | bytes accessed | tf_op | source)
XLA Modules:
  0.0 110.9 jit_solution(9212854641048557446)
XLA Ops:
  7.2 0.9 convert_reduce_fusion.1
  8.1 0.7 multiply_add_fusion
  8.9 0.8 fusion.22
  9.9 0.7 gather_fusion
  10.7 0.1 convert_element_type.30
  10.9 1.0 bitcast_bitcast_fusion
  11.9 0.6 gather_fusion.1
  12.5 0.8 fusion.6
  13.3 7.4 %all-to-all-start = ((bf16[2,16,1,16,128]{4,3,0,2,1:T(8,128)(2,1)}), bf16[2,16,1,16,128]{4,3,0,2,1:T(8,128)(2,1)S(1)}, u32[]{:S(2)}, u32[]{:S(2)}) async-start(bf16[2,16,1,16,128]{4,3,0,2,1:T(8,128)(2,1)} %fusion.6), calls=%async_computation | async-start | bytes 262144 | tf_op jit(solution)/shard_map/all_to_all | solution.py:42
  20.8 0.6 gather_fusion.5
  21.4 0.4 fusion.1
  21.8 0.5 convolution_bitcast_fusion
  22.3 3.0 %copy.55 = f32[16,72,128]{0,2,1:T(8,128)} copy(f32[16,72,128]{2,1,0:T(8,128)S(1)} %convolution_bitcast_fusion) | data formatting | bytes 1179648
  25.3 0.6 copy-done.3
  26.0 0.6 gather_fusion.2
  26.7 1.2 %copy.47 = bf16[576,1000]{0,1:T(8,128)(2,1)S(1)} copy(bf16[576,1000]{1,0:T(8,128)(2,1)S(1)} %copy-done.1) | data formatting | bytes 2304000 | tf_op args[1]
  27.9 0.6 gather_fusion.3
  28.6 22.6 %all-gather = bf16[16,576,16]{1,2,0:T(8,128)(2,1)S(1)} all-gather(bf16[1,576,16]{1,2,0:T(8,128)(2,1)S(1)} %select_bitcast_fusion), channel_id=1, replica_groups=mesh['grp'=2,'aux'=16] {'aux'}, dimensions={0}, use_global_device_ids=true | all-gather | bytes 313344 | tf_op jit(solution)/shard_map/all_gather | solution.py:29
  51.2 0.4 reshape.167
  51.7 0.6 gather_fusion.4
  52.3 0.5 fusion
  52.8 1.3 %copy.51 = bf16[2,16,128,128]{3,2,1,0:T(8,128)(2,1)} copy(bf16[2,16,128,128]{2,3,1,0:T(8,128)(2,1)S(1)} %fusion) | data formatting | bytes 2097152
  54.1 48.2 %reduce-scatter.4.cloned.1.call-done = f32[576,16]{1,0:T(8,128)} async-done(((f32[9216,16]{1,0:T(8,128)}), f32[576,16]{1,0:T(8,128)}) %reduce-scatter.4.cloned.1.call-update) | async-done | bytes 36880
  102.4 1.7 %copy.54 = f32[16,576]{1,0:T(8,128)} copy(f32[16,576]{0,1:T(8,128)} %bitcast.59) | data formatting | bytes 73728
  (34 shorter events, 1.0 us)
Async XLA Ops:
  7.2 14.2 %copy-start = (bf16[1,16,128,128]{3,2,1,0:T(8,128)(2,1)S(1)}, bf16[1,16,128,128]{3,2,1,0:T(8,128)(2,1)}, u32[]{:S(2)}) copy-start(bf16[1,16,128,128]{3,2,1,0:T(8,128)(2,1)} %param.8) | copy-start | bytes 1572868
  7.2 13.6 %copy-start.2 = (s32[16,2]{0,1:T(2,128)S(1)}, s32[16,2]{0,1:T(2,128)}, u32[]{:S(2)}) copy-start(s32[16,2]{0,1:T(2,128)} %param.10) | copy-start | bytes 388
  13.3 39.0 %all-to-all-start = ((bf16[2,16,1,16,128]{4,3,0,2,1:T(8,128)(2,1)}), bf16[2,16,1,16,128]{4,3,0,2,1:T(8,128)(2,1)S(1)}, u32[]{:S(2)}, u32[]{:S(2)}) async-start(bf16[2,16,1,16,128]{4,3,0,2,1:T(8,128)(2,1)} %fusion.6), calls=%async_computation | async-start | bytes 262144 | tf_op jit(solution)/shard_map/all_to_all | solution.py:42
  20.7 81.7 %reduce-scatter.4.cloned.1.call-start = ((), (), s32[]{:S(2)}) async-start(), calls=%async_computation.2 | async-start | bytes 5013504
  25.3 0.7 copy-start.3
  25.3 1.4 %copy-start.1 = (bf16[576,1000]{1,0:T(8,128)(2,1)S(1)}, bf16[576,1000]{1,0:T(8,128)(2,1)}, u32[]{:S(2)}) copy-start(bf16[576,1000]{1,0:T(8,128)(2,1)} %param.7) | copy-start | bytes 3456004
Sparse Core Ops, SparseCore 0:
  25.4 76.8 reduce-scatter.3
where the time goes:
time: 111 us
  waiting for transfers between devices  48.2 us (43%)
  blocking collectives  22.6 us (20%)
  between operations  14.2 us (13%)
  local copies, waits for them, and re-layouts  13.5 us (12%)
  starting transfers between devices  7.43 us (7%)
  other arithmetic  3.56 us (3%)
  matrix products  1.45 us (1%)
    unnamed x2, waiting for transfers between devices  48.2 us
    all_gather x1, blocking collectives, body(): occ_all = lax.all_gather(local_rows, 'aux', axis=0, tiled=True)  22.6 us
    unnamed x12, local copies, waits for them, and re-layouts  7.83 us
    all_to_all x1, starting transfers between devices, body(): lax.all_to_all(factor, 'aux', split_axis=1, concat_axis=1, tiled=True)  7.39 us
  transfers between devices with their start and end apart: 2, of which 1 were waited for; matrix products, arithmetic and copies ran while one was open for 9% of the time, Pallas kernels for 0%

commit v1 on v0

v1 whole, which is shorter than its diff:
```python
import functools

import jax
import jax.numpy as jnp
from jax import lax
from jax.experimental import pallas as pl
from jax.experimental.pallas import tpu as pltpu
from jax.sharding import PartitionSpec as P

SLOTS = 2
TILE = 8
UNROLL_LIMIT = 16
VMEM_BYTES = 32 * 1024 * 1024
MESH = pl.DeviceIdType.MESH


def loop(count, step, init):
    if count <= UNROLL_LIMIT:
        carry = init
        for index in range(count):
            carry = step(index, carry)
        return carry
    return lax.fori_loop(0, count, step, init)


def iota(shape, dimension):
    return lax.broadcasted_iota(jnp.int32, shape, dimension)


def exchange_kernel(
    dims,
    kept_ref,
    owner_ref,
    batch_ref,
    half_hbm,
    occ_hbm,
    integrals_hbm,
    tiles_out,
    result_out,
    half_v,
    occ_v,
    integrals_v,
    window_v,
    select_v,
    send_sums,
    recv_sums,
    send_tiles,
    send_result,
    load_sem,
    send_sem,
    recv_sem,
):
    devices, width, kept, rows, windows, edge, basis = dims
    groups = devices // width
    kept_part = kept // groups
    head = kept_part
    me = lax.axis_index("aux")
    grp = lax.axis_index("grp")
    my_group = me // width

    barrier = pltpu.get_barrier_semaphore()

    def greet(step, carry):
        peer = lax.rem(me + 1 + step, devices)
        pl.semaphore_signal(barrier, inc=1, device_id=(grp, peer), device_id_type=MESH)
        return carry

    load_half = pltpu.make_async_copy(half_hbm.at[0], half_v.at[:, pl.ds(0, basis)], load_sem.at[0])
    load_integrals = pltpu.make_async_copy(integrals_hbm.at[0], integrals_v, load_sem.at[1])
    load_occ = pltpu.make_async_copy(occ_hbm, occ_v, load_sem.at[2])
    load_half.start()
    load_integrals.start()
    load_occ.start()
    loop(devices - 1, greet, 0)

    half_v[:, pl.ds(basis, edge)] = jnp.zeros((width, edge), half_v.dtype)
    window_v[...] = jnp.zeros_like(window_v)

    split_lanes = 3 * kept_part
    lane_kept = lax.rem(iota((TILE, split_lanes), 1), kept_part)
    row_lane = jnp.full((TILE, split_lanes), -1, jnp.int32)
    for index in range(kept_part):
        row_lane = jnp.where(lane_kept == index, kept_ref[my_group * kept_part + index, 0], row_lane)
    lane_window = iota((TILE, devices * TILE), 1)
    window_index = lax.rem(lane_window, TILE)
    window_block = jnp.where(
        window_index < windows, ((lane_window // TILE) * rows) // edge + window_index, -5
    )
    sub_kept = iota((TILE, split_lanes), 0)
    sub_window = iota((TILE, devices * TILE), 0)

    load_half.wait()

    def place(dest, carry):
        def scan(step, found):
            index = kept - 1 - step
            col_a, row_a, col_b, row_b = found
            hit = owner_ref[index] == dest
            return (
                jnp.where(hit, kept_ref[index, 1], col_a),
                jnp.where(hit, kept_ref[index, 0], row_a),
                jnp.where(hit, col_a, col_b),
                jnp.where(hit, row_a, row_b),
            )

        col_a, row_a, col_b, row_b = loop(
            kept, scan, (jnp.int32(basis // edge), jnp.int32(-1), jnp.int32(basis // edge), jnp.int32(-1))
        )
        send_tiles[dest, pl.ds(0, width), :] = half_v[:, pl.ds(col_a * edge, edge)]
        send_tiles[dest, pl.ds(width, width), :] = half_v[:, pl.ds(col_b * edge, edge)]
        if groups > 1:
            mine = lax.rem(dest, groups) == my_group
            row_a = jnp.where(mine, row_a, -1)
            row_b = jnp.where(mine, row_b, -1)
        wanted = jnp.where(sub_window == windows, row_a, jnp.where(sub_window == windows + 1, row_b, -1))
        pick_occ = jnp.where(wanted == window_block, 1.0, 0.0)
        block = jnp.where(sub_kept < windows, (dest * rows) // edge + sub_kept, -5)
        pick_sum = jnp.where(block == row_lane, 1.0, 0.0)
        select_v[dest] = jnp.concatenate([pick_occ, pick_sum], axis=1)
        return carry

    loop(devices, place, 0)

    load_integrals.wait()
    for index in range(kept):
        group, place_in = index // kept_part, index % kept_part
        start = kept_ref[index, 1] * edge
        piece = lax.dot_general(
            half_v[:, pl.ds(start, edge)],
            integrals_v[index],
            (((1,), (1,)), ((), ())),
            preferred_element_type=jnp.float32,
        )
        send_sums[pl.ds(group * width, width), place_in, :] = piece

    load_occ.wait()
    orbitals = occ_v.shape[1]
    sub_batch = iota((width, 1), 0)
    batch = jnp.zeros((width, 1), jnp.int32)
    for index in range(width):
        batch = jnp.where(sub_batch == index, batch_ref[index], batch)
    pick = jnp.where(iota((width, orbitals), 1) == batch, 1.0, 0.0).astype(jnp.bfloat16)
    window_v[:, pl.ds(0, rows)] = lax.dot_general(
        pick, occ_v[...], (((1,), (1,)), ((), ())), preferred_element_type=jnp.float32
    )
    shifted = pltpu.roll(window_v[...], lax.rem(me * rows, edge), 1)
    for group in range(groups):
        for index in range(windows):
            send_sums[pl.ds(group * width, width), head + index, :] = shifted[
                :, index * edge : (index + 1) * edge
            ]
        for index in range(windows, TILE):
            send_sums[pl.ds(group * width, width), head + index, :] = jnp.zeros(
                (width, edge), jnp.float32
            )

    def sums_copy(peer):
        return pltpu.make_async_remote_copy(
            src_ref=send_sums.at[peer],
            dst_ref=recv_sums.at[me],
            send_sem=send_sem.at[0],
            recv_sem=recv_sem.at[0],
            device_id=(grp, peer),
            device_id_type=MESH,
        )

    def tiles_copy(peer):
        return pltpu.make_async_remote_copy(
            src_ref=send_tiles.at[peer],
            dst_ref=tiles_out.at[me],
            send_sem=send_sem.at[1],
            recv_sem=recv_sem.at[1],
            device_id=(grp, peer),
            device_id_type=MESH,
        )

    def result_copy(peer):
        return pltpu.make_async_remote_copy(
            src_ref=send_result.at[peer],
            dst_ref=result_out.at[me],
            send_sem=send_sem.at[2],
            recv_sem=recv_sem.at[2],
            device_id=(grp, peer),
            device_id_type=MESH,
        )

    def start_all(copy):
        def start(step, carry):
            copy(lax.rem(me + 1 + step, devices)).start()
            return carry

        loop(devices - 1, start, 0)

    def wait_all(buffer, sem):
        others = buffer.at[pl.ds(0, devices - 1)]
        pltpu.make_async_copy(others, others, sem).wait()

    pl.semaphore_wait(barrier, devices - 1)
    start_all(sums_copy)
    start_all(tiles_copy)
    recv_sums[me] = send_sums[me]
    tiles_out[me] = send_tiles[me]
    wait_all(recv_sums, recv_sem.at[0])

    total = jnp.sum(recv_sums[:, pl.ds(0, head), :], axis=0)
    high = total.astype(jnp.bfloat16)
    left = total - high.astype(jnp.float32)
    middle = left.astype(jnp.bfloat16)
    low = (left - middle.astype(jnp.float32)).astype(jnp.bfloat16)
    window_rows = recv_sums[:, pl.ds(head, TILE), :].reshape(devices * TILE, edge).astype(jnp.bfloat16)
    operand = jnp.concatenate([window_rows, high, middle, low], axis=0)
    select = select_v[...].reshape(devices * TILE, devices * TILE + split_lanes).astype(jnp.bfloat16)
    moved = jnp.dot(select, operand, preferred_element_type=jnp.float32)
    send_result[...] = moved.reshape(devices, TILE, edge)
    start_all(result_copy)
    result_out[me] = send_result[me]
    wait_all(tiles_out, recv_sem.at[1])
    wait_all(result_out, recv_sem.at[2])
    wait_all(send_sums, send_sem.at[0])
    wait_all(send_tiles, send_sem.at[1])
    wait_all(send_result, send_sem.at[2])


def finish_kernel(dims, tiles_ref, result_ref, blocks_hbm, lagrangian_ref, blocks_v, store_sem):
    devices, width, kept, rows, windows, edge, basis = dims
    me = lax.axis_index("aux")

    def row(index):
        return jnp.sum(result_ref[:, index, :].reshape(devices // width, width, edge), axis=0)

    for slot in range(SLOTS):
        left = row(windows + slot).T.astype(jnp.bfloat16)

        def form(index, carry):
            blocks_v[slot, index] = jnp.dot(
                left,
                tiles_ref[index, pl.ds(slot * width, width), :],
                preferred_element_type=jnp.float32,
            ).astype(jnp.bfloat16)
            return carry

        loop(devices, form, 0)
        pltpu.make_async_copy(blocks_v.at[slot], blocks_hbm.at[slot], store_sem.at[slot]).start()
    whole = jnp.concatenate([row(index) for index in range(windows)], axis=1)
    offset = lax.rem(me * rows, edge)
    whole = pltpu.roll(whole, lax.rem(windows * edge - offset, windows * edge), 1)
    lagrangian_ref[...] = whole[:, :rows]
    for slot in range(SLOTS):
        pltpu.make_async_copy(blocks_v.at[slot], blocks_hbm.at[slot], store_sem.at[slot]).wait()


def body(gamma_half, c_occ, integrals, occ_batch, kept_blocks, block_owner):
    devices = lax.axis_size("aux")
    aux_dev, width, basis = gamma_half.shape
    kept, edge = integrals.shape[1], integrals.shape[-1]
    rows, orbitals = c_occ.shape
    windows = max((index * rows % edge + rows + edge - 1) // edge for index in range(devices))
    assert aux_dev == 1 and devices % width == 0 and kept % (devices // width) == 0
    assert windows + SLOTS <= TILE
    dims = (devices, width, kept, rows, windows, edge, basis)
    kept_part = kept * width // devices
    sums = (devices, kept_part + TILE, edge)
    tiles = (devices, SLOTS * width, edge)
    result = (devices, TILE, edge)
    smem = pl.BlockSpec(memory_space=pltpu.SMEM)
    vmem = pl.BlockSpec(memory_space=pltpu.VMEM)
    anywhere = pl.BlockSpec(memory_space=pl.ANY)
    received, moved = pl.pallas_call(
        functools.partial(exchange_kernel, dims),
        out_shape=(
            jax.ShapeDtypeStruct(tiles, jnp.bfloat16),
            jax.ShapeDtypeStruct(result, jnp.float32),
        ),
        in_specs=[smem, smem, smem, anywhere, anywhere, anywhere],
        out_specs=(vmem, vmem),
        scratch_shapes=[
            pltpu.VMEM((width, basis + edge), jnp.bfloat16),
            pltpu.VMEM((rows, orbitals), jnp.bfloat16),
            pltpu.VMEM((kept, edge, edge), jnp.bfloat16),
            pltpu.VMEM((width, windows * edge), jnp.float32),
            pltpu.VMEM((devices, TILE, devices * TILE + 3 * kept_part), jnp.float32),
            pltpu.VMEM(sums, jnp.float32),
            pltpu.VMEM(sums, jnp.float32),
            pltpu.VMEM(tiles, jnp.bfloat16),
            pltpu.VMEM(result, jnp.float32),
            pltpu.SemaphoreType.DMA((3,)),
            pltpu.SemaphoreType.DMA((3,)),
            pltpu.SemaphoreType.DMA((3,)),
        ],
        compiler_params=pltpu.CompilerParams(
            collective_id=0, has_side_effects=True, vmem_limit_bytes=VMEM_BYTES
        ),
        name="exchange",
    )(kept_blocks, block_owner, occ_batch, gamma_half, c_occ, integrals)
    return pl.pallas_call(
        functools.partial(finish_kernel, dims),
        out_shape=(
            jax.ShapeDtypeStruct((SLOTS, devices, edge, edge), jnp.bfloat16),
            jax.ShapeDtypeStruct((width, rows), jnp.float32),
        ),
        in_specs=[vmem, vmem],
        out_specs=(anywhere, vmem),
        scratch_shapes=[
            pltpu.VMEM((SLOTS, devices, edge, edge), jnp.bfloat16),
            pltpu.SemaphoreType.DMA((SLOTS,)),
        ],
        compiler_params=pltpu.CompilerParams(vmem_limit_bytes=VMEM_BYTES),
        name="finish",
    )(received, moved)


def solution(mesh):
    return jax.shard_map(
        body,
        mesh=mesh,
        in_specs=(
            P(("grp", "aux"), None, None),
            P(("grp", "aux"), None),
            P(("grp", "aux"), None, None, None),
            P("grp"),
            P("grp", None),
            P("grp"),
        ),
        out_specs=(P(("grp", "aux"), None, None, None), P("grp", "aux")),
        check_vma=False,
    )
```

time: 111 us -> 26.6 us (0.24)
  waiting for transfers between devices: 48.2 us -> 0 us
  blocking collectives: 22.6 us -> 0 us
  Pallas kernels: 0 us -> 20.3 us
  between operations: 14.2 us -> 0.64 us
  local copies, waits for them, and re-layouts: 13.5 us -> 5.34 us
  starting transfers between devices: 7.43 us -> 0 us
  other arithmetic: 3.56 us -> 0 us
  matrix products: 1.45 us -> 0 us
    unnamed x2 -> x0, waiting for transfers between devices: 48.2 us -> none
    all_gather x1 -> x0, blocking collectives: 22.6 us -> none  [body(): occ_all = lax.all_gather(local_rows, 'aux', axis=0, tiled=True)]
    pallas_call x0 -> x2, Pallas kernels: none -> 20.3 us  [the longest x1 18.4 us: body(): pl.pallas_call(functools.partial(exchange_kernel, dims), out_shape=(jax.S...]
    all_to_all x1 -> x0, starting transfers between devices: 7.39 us -> none  [body(): lax.all_to_all(factor, 'aux', split_axis=1, concat_axis=1, tiled=True)]
    gather x8 -> x0, local copies, waits for them, and re-layouts: 3.82 us -> none  [the longest x2 1.2 us: body(): own_tiles = jnp.take(occ_tiles, jnp.take(row_blocks, own_blocks), axis=0)]
    unnamed x12 -> x11, local copies, waits for them, and re-layouts: 7.83 us -> 5.34 us
    dot_general x3 -> x0, matrix products: 1.45 us -> none  [the longest x1 0.53 us: body(): jnp.einsum('sxb,spby->spxy', own_tiles, received, preferred_element_type=...]
  transfers between devices with their start and end apart: 2 -> 0, of which waited for: 1 -> 0; matrix products, arithmetic and copies ran while one was open for 9% -> 0% of each run, Pallas kernels for 0% -> 0%
where the time goes in v1:
time: 26.6 us; the launch traced here: 26.3 us
  Pallas kernels  20.3 us (76%)
  local copies, waits for them, and re-layouts  5.34 us (20%)
  between operations  0.64 us (2%)
    pallas_call x1, Pallas kernels, body(): pl.pallas_call(functools.partial(exchange_kernel, dims), out_shape=(jax.S...  18.4 us
    unnamed x11, local copies, waits for them, and re-layouts  5.34 us
    pallas_call x1, Pallas kernels, body(): pl.pallas_call(functools.partial(finish_kernel, dims), out_shape=(jax.Sha...  1.95 us

profile of v1, /device:TPU:0, one launch (start us, length us, event | category | flops | bytes accessed | tf_op | source)
XLA Modules:
  0.0 26.3 jit_solution(15059927336537304027)
XLA Ops:
  0.6 0.8 %copy.8.kept_ref = s32[16,2]{1,0:T(8,128)S(1)} copy(s32[16,2]{0,1:T(2,128)} %param.10) | data formatting | bytes 256 | tf_op args[4]
  1.4 0.0 copy-start
  1.4 1.3 %copy-done = bf16[576,1000]{1,0:T(8,128)(2,1)S(1)} copy-done((bf16[576,1000]{1,0:T(8,128)(2,1)S(1)}, bf16[576,1000]{1,0:T(8,128)(2,1)}, u32[]{:S(2)}) %copy-start) | copy-done | bytes 1152024
  2.7 0.0 copy-start.1
  2.7 1.0 %copy-done.1 = bf16[1,16,128,128]{3,2,1,0:T(8,128)(2,1)S(1)} copy-done((bf16[1,16,128,128]{3,2,1,0:T(8,128)(2,1)S(1)}, bf16[1,16,128,128]{3,2,1,0:T(8,128)(2,1)}, u32[]{:S(2)}) %copy-start.1) | copy-done | bytes 524312
  3.7 0.0 copy-start.2
  3.7 1.0 %copy-done.2 = bf16[1,16,9216]{2,1,0:T(8,128)(2,1)S(1)} copy-done((bf16[1,16,9216]{2,1,0:T(8,128)(2,1)S(1)}, bf16[1,16,9216]{2,1,0:T(8,128)(2,1)}, u32[]{:S(2)}) %copy-start.2) | copy-done | bytes 294936
  4.7 0.0 copy-start.3
  4.7 0.7 %copy-done.3 = s32[16]{0:T(128)S(1)} copy-done((s32[16]{0:T(128)S(1)}, s32[16]{0:T(128)}, u32[]{:S(2)}) %copy-start.3) | copy-done | bytes 88
  5.3 0.0 copy-start.4
  5.3 0.7 %copy-done.4 = s32[16]{0:T(128)S(1)} copy-done((s32[16]{0:T(128)S(1)}, s32[16]{0:T(128)}, u32[]{:S(2)}) %copy-start.4) | copy-done | bytes 88
  6.0 18.4 %exchange.1 = (bf16[16,32,128]{2,1,0:T(8,128)(2,1)S(1)}, f32[16,8,128]{2,1,0:T(8,128)S(1)}) custom-call(s32[16,2]{1,0:T(8,128)S(1)} %copy.8.kept_ref, s32[16]{0:T(128)S(1)} %copy-done.3, s32[16]{0:T(128)S(1)} %copy-done.4, bf16[1,16,9216]{2,1,0:T(8,128)(2,1)S(1)} %copy-done.2, bf16[576,1000]{1,0:T(8,128)(2,1)S(1)} %copy-done, ...), custom_call_target="tpu_custom_call" | custom-call | tf_op jit(solution)/shard_map/exchange/pallas_call | solution.py:268
  24.3 2.0 %finish.1 = (bf16[2,16,128,128]{3,2,1,0:T(8,128)(2,1)}, f32[16,576]{1,0:T(8,128)}) custom-call(bf16[16,32,128]{2,1,0:T(8,128)(2,1)S(1)} %get-tuple-element.4.tiles_ref, f32[16,8,128]{2,1,0:T(8,128)S(1)} %get-tuple-element.5.result_ref), custom_call_target="tpu_custom_call" | custom-call | tf_op jit(solution)/shard_map/finish/pallas_call | solution.py:295
Async XLA Ops:
  1.4 1.3 %copy-start = (bf16[576,1000]{1,0:T(8,128)(2,1)S(1)}, bf16[576,1000]{1,0:T(8,128)(2,1)}, u32[]{:S(2)}) copy-start(bf16[576,1000]{1,0:T(8,128)(2,1)} %occ_hbm.1) | copy-start | bytes 3456004
  2.7 1.0 %copy-start.1 = (bf16[1,16,128,128]{3,2,1,0:T(8,128)(2,1)S(1)}, bf16[1,16,128,128]{3,2,1,0:T(8,128)(2,1)}, u32[]{:S(2)}) copy-start(bf16[1,16,128,128]{3,2,1,0:T(8,128)(2,1)} %integrals_hbm.1) | copy-start | bytes 1572868
  3.7 1.0 %copy-start.2 = (bf16[1,16,9216]{2,1,0:T(8,128)(2,1)S(1)}, bf16[1,16,9216]{2,1,0:T(8,128)(2,1)}, u32[]{:S(2)}) copy-start(bf16[1,16,9216]{2,1,0:T(8,128)(2,1)} %half_hbm.1) | copy-start | bytes 884740
  4.7 0.7 %copy-start.3 = (s32[16]{0:T(128)S(1)}, s32[16]{0:T(128)}, u32[]{:S(2)}) copy-start(s32[16]{0:T(128)} %owner_ref.1) | copy-start | bytes 196
  5.3 0.7 %copy-start.4 = (s32[16]{0:T(128)S(1)}, s32[16]{0:T(128)}, u32[]{:S(2)}) copy-start(s32[16]{0:T(128)} %batch_ref.1) | copy-start | bytes 196

commit v2 on v1

--- a/solution.py
+++ b/solution.py
@@ -10,7 +10,7 @@
 SLOTS = 2
 TILE = 8
 UNROLL_LIMIT = 16
-VMEM_BYTES = 32 * 1024 * 1024
+VMEM_BYTES = 60 * 1024 * 1024
 MESH = pl.DeviceIdType.MESH
 
 
@@ -29,14 +29,17 @@
 
 def exchange_kernel(
     dims,
-    kept_ref,
-    owner_ref,
-    batch_ref,
+    kept_hbm,
+    owner_hbm,
+    batch_hbm,
     half_hbm,
     occ_hbm,
     integrals_hbm,
     tiles_out,
     result_out,
+    kept_ref,
+    owner_ref,
+    batch_ref,
     half_v,
     occ_v,
     integrals_v,
@@ -65,6 +68,12 @@
         pl.semaphore_signal(barrier, inc=1, device_id=(grp, peer), device_id_type=MESH)
         return carry
 
+    load_kept = pltpu.make_async_copy(kept_hbm, kept_ref, load_sem.at[3])
+    load_owner = pltpu.make_async_copy(owner_hbm, owner_ref, load_sem.at[4])
+    load_batch = pltpu.make_async_copy(batch_hbm, batch_ref, load_sem.at[5])
+    load_kept.start()
+    load_owner.start()
+    load_batch.start()
     load_half = pltpu.make_async_copy(half_hbm.at[0], half_v.at[:, pl.ds(0, basis)], load_sem.at[0])
     load_integrals = pltpu.make_async_copy(integrals_hbm.at[0], integrals_v, load_sem.at[1])
     load_occ = pltpu.make_async_copy(occ_hbm, occ_v, load_sem.at[2])
@@ -76,11 +85,15 @@
     half_v[:, pl.ds(basis, edge)] = jnp.zeros((width, edge), half_v.dtype)
     window_v[...] = jnp.zeros_like(window_v)
 
+    load_kept.wait()
+    load_owner.wait()
+    load_batch.wait()
+
     split_lanes = 3 * kept_part
     lane_kept = lax.rem(iota((TILE, split_lanes), 1), kept_part)
     row_lane = jnp.full((TILE, split_lanes), -1, jnp.int32)
     for index in range(kept_part):
-        row_lane = jnp.where(lane_kept == index, kept_ref[my_group * kept_part + index, 0], row_lane)
+        row_lane = jnp.where(lane_kept == index, kept_ref[0, my_group * kept_part + index], row_lane)
     lane_window = iota((TILE, devices * TILE), 1)
     window_index = lax.rem(lane_window, TILE)
     window_block = jnp.where(
@@ -97,8 +110,8 @@
             col_a, row_a, col_b, row_b = found
             hit = owner_ref[index] == dest
             return (
-                jnp.where(hit, kept_ref[index, 1], col_a),
-                jnp.where(hit, kept_ref[index, 0], row_a),
+                jnp.where(hit, kept_ref[1, index], col_a),
+                jnp.where(hit, kept_ref[0, index], row_a),
                 jnp.where(hit, col_a, col_b),
                 jnp.where(hit, row_a, row_b),
             )
@@ -124,7 +137,7 @@
     load_integrals.wait()
     for index in range(kept):
         group, place_in = index // kept_part, index % kept_part
-        start = kept_ref[index, 1] * edge
+        start = kept_ref[1, index] * edge
         piece = lax.dot_general(
             half_v[:, pl.ds(start, edge)],
             integrals_v[index],
@@ -262,7 +275,7 @@
     sums = (devices, kept_part + TILE, edge)
     tiles = (devices, SLOTS * width, edge)
     result = (devices, TILE, edge)
-    smem = pl.BlockSpec(memory_space=pltpu.SMEM)
+    hbm = pl.BlockSpec(memory_space=pltpu.HBM)
     vmem = pl.BlockSpec(memory_space=pltpu.VMEM)
     anywhere = pl.BlockSpec(memory_space=pl.ANY)
     received, moved = pl.pallas_call(
@@ -271,9 +284,12 @@
             jax.ShapeDtypeStruct(tiles, jnp.bfloat16),
             jax.ShapeDtypeStruct(result, jnp.float32),
         ),
-        in_specs=[smem, smem, smem, anywhere, anywhere, anywhere],
+        in_specs=[hbm] * 6,
         out_specs=(vmem, vmem),
         scratch_shapes=[
+            pltpu.SMEM((2, kept), jnp.int32),
+            pltpu.SMEM((kept,), jnp.int32),
+            pltpu.SMEM((width,), jnp.int32),
             pltpu.VMEM((width, basis + edge), jnp.bfloat16),
             pltpu.VMEM((rows, orbitals), jnp.bfloat16),
             pltpu.VMEM((kept, edge, edge), jnp.bfloat16),
@@ -283,7 +299,7 @@
             pltpu.VMEM(sums, jnp.float32),
             pltpu.VMEM(tiles, jnp.bfloat16),
             pltpu.VMEM(result, jnp.float32),
-            pltpu.SemaphoreType.DMA((3,)),
+            pltpu.SemaphoreType.DMA((6,)),
             pltpu.SemaphoreType.DMA((3,)),
             pltpu.SemaphoreType.DMA((3,)),
         ],
@@ -291,7 +307,7 @@
             collective_id=0, has_side_effects=True, vmem_limit_bytes=VMEM_BYTES
         ),
         name="exchange",
-    )(kept_blocks, block_owner, occ_batch, gamma_half, c_occ, integrals)
+    )(kept_blocks.T, block_owner, occ_batch, gamma_half, c_occ, integrals)
     return pl.pallas_call(
         functools.partial(finish_kernel, dims),
         out_shape=(

time: 26.6 us -> 21.8 us (0.82)
  local copies, waits for them, and re-layouts: 5.34 us -> 0 us
  Pallas kernels: 20.3 us -> 21 us
    unnamed x11 -> x0, local copies, waits for them, and re-layouts: 5.34 us -> none
    pallas_call x1, Pallas kernels: 1.95 us -> 2.86 us  [body(): pl.pallas_call(functools.partial(finish_kernel, dims), out_shape=(jax.Sha...]
    pallas_call x1, Pallas kernels: 18.4 us -> 18.1 us  [body(): pl.pallas_call(functools.partial(exchange_kernel, dims), out_shape=(jax.S...]
where the time goes in v2:
time: 21.8 us; the launch traced here: 21.6 us
  Pallas kernels  21 us (96%)
  between operations  0.64 us (3%)
    pallas_call x1, Pallas kernels, body(): pl.pallas_call(functools.partial(exchange_kernel, dims), out_shape=(jax.S...  18.1 us
    pallas_call x1, Pallas kernels, body(): pl.pallas_call(functools.partial(finish_kernel, dims), out_shape=(jax.Sha...  2.86 us

profile of v2, /device:TPU:0, one launch (start us, length us, event | category | flops | bytes accessed | tf_op | source)
XLA Modules:
  0.0 21.6 jit_solution(16887869566212561540)
XLA Ops:
  0.6 18.1 %exchange.1 = (bf16[16,32,128]{2,1,0:T(8,128)(2,1)}, f32[16,8,128]{2,1,0:T(8,128)}) custom-call(s32[2,16]{1,0:T(2,128)} %bitcast.1, s32[16]{0:T(128)} %owner_hbm.1, s32[16]{0:T(128)} %batch_hbm.1, bf16[1,16,9216]{2,1,0:T(8,128)(2,1)} %half_hbm.1, bf16[576,1000]{1,0:T(8,128)(2,1)} %occ_hbm.1, bf16[1,16,128,128]{3,2,1,0:T(8,128)(2,1)} %integrals_hbm.1), custom_call_target="tpu_custom_call" | custom-call | tf_op jit(solution)/shard_map/exchange/pallas_call | solution.py:281
  18.7 2.9 %finish.1 = (bf16[2,16,128,128]{3,2,1,0:T(8,128)(2,1)}, f32[16,576]{1,0:T(8,128)}) custom-call(bf16[16,32,128]{2,1,0:T(8,128)(2,1)} %get-tuple-element.4.tiles_ref, f32[16,8,128]{2,1,0:T(8,128)} %get-tuple-element.5.result_ref), custom_call_target="tpu_custom_call" | custom-call | tf_op jit(solution)/shard_map/finish/pallas_call | solution.py:311

commit v3 on v2

--- a/solution.py
+++ b/solution.py
@@ -104,7 +104,7 @@
 
     load_half.wait()
 
-    def place(dest, carry):
+    def owned(dest):
         def scan(step, found):
             index = kept - 1 - step
             col_a, row_a, col_b, row_b = found
@@ -116,11 +116,20 @@
                 jnp.where(hit, row_a, row_b),
             )
 
-        col_a, row_a, col_b, row_b = loop(
-            kept, scan, (jnp.int32(basis // edge), jnp.int32(-1), jnp.int32(basis // edge), jnp.int32(-1))
-        )
+        return loop(
+            kept,
+            scan,
+            (jnp.int32(basis // edge), jnp.int32(-1), jnp.int32(basis // edge), jnp.int32(-1)),
+        )
+
+    def fill_tiles(dest, carry):
+        col_a, _, col_b, _ = owned(dest)
         send_tiles[dest, pl.ds(0, width), :] = half_v[:, pl.ds(col_a * edge, edge)]
         send_tiles[dest, pl.ds(width, width), :] = half_v[:, pl.ds(col_b * edge, edge)]
+        return carry
+
+    def fill_select(dest, carry):
+        _, row_a, _, row_b = owned(dest)
         if groups > 1:
             mine = lax.rem(dest, groups) == my_group
             row_a = jnp.where(mine, row_a, -1)
@@ -131,8 +140,6 @@
         pick_sum = jnp.where(block == row_lane, 1.0, 0.0)
         select_v[dest] = jnp.concatenate([pick_occ, pick_sum], axis=1)
         return carry
-
-    loop(devices, place, 0)
 
     load_integrals.wait()
     for index in range(kept):
@@ -210,7 +217,9 @@
 
     pl.semaphore_wait(barrier, devices - 1)
     start_all(sums_copy)
+    loop(devices, fill_tiles, 0)
     start_all(tiles_copy)
+    loop(devices, fill_select, 0)
     recv_sums[me] = send_sums[me]
     tiles_out[me] = send_tiles[me]
     wait_all(recv_sums, recv_sem.at[0])
@@ -281,8 +290,8 @@
     received, moved = pl.pallas_call(
         functools.partial(exchange_kernel, dims),
         out_shape=(
-            jax.ShapeDtypeStruct(tiles, jnp.bfloat16),
-            jax.ShapeDtypeStruct(result, jnp.float32),
+            pltpu.VMEM(tiles, jnp.bfloat16),
+            pltpu.VMEM(result, jnp.float32),
         ),
         in_specs=[hbm] * 6,
         out_specs=(vmem, vmem),
@@ -320,7 +329,7 @@
             pltpu.VMEM((SLOTS, devices, edge, edge), jnp.bfloat16),
             pltpu.SemaphoreType.DMA((SLOTS,)),
         ],
-        compiler_params=pltpu.CompilerParams(vmem_limit_bytes=VMEM_BYTES),
+        compiler_params=pltpu.CompilerParams(vmem_limit_bytes=VMEM_BYTES // 2),
         name="finish",
     )(received, moved)
 

time: 21.8 us -> 20.2 us (0.927)
  Pallas kernels: 21 us -> 19.4 us
    pallas_call x1, Pallas kernels: 2.86 us -> 1.96 us  [body(): pl.pallas_call(functools.partial(finish_kernel, dims), out_shape=(jax.Sha...]
    pallas_call x1, Pallas kernels: 18.1 us -> 17.4 us  [body(): pl.pallas_call(functools.partial(exchange_kernel, dims), out_shape=(pltpu...]
where the time goes in v3:
time: 20.2 us; the launch traced here: 20 us
  Pallas kernels  19.4 us (96%)
  between operations  0.64 us (3%)
    pallas_call x1, Pallas kernels, body(): pl.pallas_call(functools.partial(exchange_kernel, dims), out_shape=(pltpu...  17.4 us
    pallas_call x1, Pallas kernels, body(): pl.pallas_call(functools.partial(finish_kernel, dims), out_shape=(jax.Sha...  1.96 us

profile of v3, /device:TPU:0, one launch (start us, length us, event | category | flops | bytes accessed | tf_op | source)
XLA Modules:
  0.0 20.0 jit_solution(4147175427070526096)
XLA Ops:
  0.6 17.4 %exchange.1 = (bf16[16,32,128]{2,1,0:T(8,128)(2,1)S(1)}, f32[16,8,128]{2,1,0:T(8,128)S(1)}) custom-call(s32[2,16]{1,0:T(2,128)} %bitcast.1, s32[16]{0:T(128)} %owner_hbm.1, s32[16]{0:T(128)} %batch_hbm.1, bf16[1,16,9216]{2,1,0:T(8,128)(2,1)} %half_hbm.1, bf16[576,1000]{1,0:T(8,128)(2,1)} %occ_hbm.1, bf16[1,16,128,128]{3,2,1,0:T(8,128)(2,1)} %integrals_hbm.1), custom_call_target="tpu_custom_call" | custom-call | tf_op jit(solution)/shard_map/exchange/pallas_call | solution.py:290
  18.1 2.0 %finish.1 = (bf16[2,16,128,128]{3,2,1,0:T(8,128)(2,1)}, f32[16,576]{1,0:T(8,128)}) custom-call(bf16[16,32,128]{2,1,0:T(8,128)(2,1)S(1)} %get-tuple-element.4.tiles_ref, f32[16,8,128]{2,1,0:T(8,128)S(1)} %get-tuple-element.5.result_ref), custom_call_target="tpu_custom_call" | custom-call | tf_op jit(solution)/shard_map/finish/pallas_call | solution.py:320

commit v4 on v3

--- a/solution.py
+++ b/solution.py
@@ -9,6 +9,7 @@
 
 SLOTS = 2
 TILE = 8
+PARTS = 2
 UNROLL_LIMIT = 16
 VMEM_BYTES = 60 * 1024 * 1024
 MESH = pl.DeviceIdType.MESH
@@ -250,25 +251,35 @@
     def row(index):
         return jnp.sum(result_ref[:, index, :].reshape(devices // width, width, edge), axis=0)
 
+    def store(slot, part):
+        span = pl.ds(part * (devices // PARTS), devices // PARTS)
+        return pltpu.make_async_copy(
+            blocks_v.at[slot, span], blocks_hbm.at[slot, span], store_sem.at[slot * PARTS + part]
+        )
+
     for slot in range(SLOTS):
         left = row(windows + slot).T.astype(jnp.bfloat16)
 
-        def form(index, carry):
-            blocks_v[slot, index] = jnp.dot(
-                left,
-                tiles_ref[index, pl.ds(slot * width, width), :],
-                preferred_element_type=jnp.float32,
-            ).astype(jnp.bfloat16)
+        def form(pair, carry):
+            right = jnp.concatenate(
+                [tiles_ref[2 * pair + half, pl.ds(slot * width, width), :] for half in range(2)], axis=1
+            )
+            both = jnp.dot(left, right, preferred_element_type=jnp.float32).astype(jnp.bfloat16)
+            for half in range(2):
+                blocks_v[slot, 2 * pair + half] = both[:, half * edge : (half + 1) * edge]
             return carry
 
-        loop(devices, form, 0)
-        pltpu.make_async_copy(blocks_v.at[slot], blocks_hbm.at[slot], store_sem.at[slot]).start()
+        for part in range(PARTS):
+            pairs = devices // 2 // PARTS
+            loop(pairs, lambda step, carry: form(part * pairs + step, carry), 0)
+            store(slot, part).start()
     whole = jnp.concatenate([row(index) for index in range(windows)], axis=1)
     offset = lax.rem(me * rows, edge)
     whole = pltpu.roll(whole, lax.rem(windows * edge - offset, windows * edge), 1)
     lagrangian_ref[...] = whole[:, :rows]
     for slot in range(SLOTS):
-        pltpu.make_async_copy(blocks_v.at[slot], blocks_hbm.at[slot], store_sem.at[slot]).wait()
+        for part in range(PARTS):
+            store(slot, part).wait()
 
 
 def body(gamma_half, c_occ, integrals, occ_batch, kept_blocks, block_owner):
@@ -327,7 +338,7 @@
         out_specs=(anywhere, vmem),
         scratch_shapes=[
             pltpu.VMEM((SLOTS, devices, edge, edge), jnp.bfloat16),
-            pltpu.SemaphoreType.DMA((SLOTS,)),
+            pltpu.SemaphoreType.DMA((SLOTS * PARTS,)),
         ],
         compiler_params=pltpu.CompilerParams(vmem_limit_bytes=VMEM_BYTES // 2),
         name="finish",

time: 20.2 us -> 20.1 us (level)
  no operation moved by 1% of the time
where the time goes in v4:
time: 20.1 us; the launch traced here: 19.9 us
  Pallas kernels  19.3 us (96%)
  between operations  0.64 us (3%)
    pallas_call x1, Pallas kernels, body(): pl.pallas_call(functools.partial(exchange_kernel, dims), out_shape=(pltpu...  17.4 us
    pallas_call x1, Pallas kernels, body(): pl.pallas_call(functools.partial(finish_kernel, dims), out_shape=(jax.Sha...  1.89 us

profile of v4, /device:TPU:0, one launch (start us, length us, event | category | flops | bytes accessed | tf_op | source)
XLA Modules:
  0.0 19.9 jit_solution(17946664063672770232)
XLA Ops:
  0.6 17.4 %exchange.1 = (bf16[16,32,128]{2,1,0:T(8,128)(2,1)S(1)}, f32[16,8,128]{2,1,0:T(8,128)S(1)}) custom-call(s32[2,16]{1,0:T(2,128)} %bitcast.1, s32[16]{0:T(128)} %owner_hbm.1, s32[16]{0:T(128)} %batch_hbm.1, bf16[1,16,9216]{2,1,0:T(8,128)(2,1)} %half_hbm.1, bf16[576,1000]{1,0:T(8,128)(2,1)} %occ_hbm.1, bf16[1,16,128,128]{3,2,1,0:T(8,128)(2,1)} %integrals_hbm.1), custom_call_target="tpu_custom_call" | custom-call | tf_op jit(solution)/shard_map/exchange/pallas_call | solution.py:301
  18.1 1.9 %finish.1 = (bf16[2,16,128,128]{3,2,1,0:T(8,128)(2,1)}, f32[16,576]{1,0:T(8,128)}) custom-call(bf16[16,32,128]{2,1,0:T(8,128)(2,1)S(1)} %get-tuple-element.4.tiles_ref, f32[16,8,128]{2,1,0:T(8,128)S(1)} %get-tuple-element.5.result_ref), custom_call_target="tpu_custom_call" | custom-call | tf_op jit(solution)/shard_map/finish/pallas_call | solution.py:331
